TPU v7x, 256 devices: a whole 4x4x8 slice. The times are simulated.
256 devices in a mesh: tm: 64 (over z, y, core), heads: 4 (over x).
Axes of the slice: x: 4, y: 4, z: 8, core: 2. Of those that a mesh axis runs over, the one named last changes fastest.
Arguments:
- video: bfloat16 [128, 196, 768], P('tm'), may hold values from -12 to 12
- t_gain: float32 [768], replicated, may hold values from 0.1 to 1.9
- t_qkv: bfloat16 [3, 768, 768], P(None, 'heads'), may hold values from -3 to 3
- t_out: bfloat16 [768, 768], P('heads'), may hold values from -0.21875 to 0.21875
- s_gain: float32 [768], replicated, may hold values from 0.1 to 1.9
- s_qkv: bfloat16 [3, 768, 768], P(None, 'heads'), may hold values from -3 to 3
- s_out: bfloat16 [768, 768], P('heads'), may hold values from -0.21875 to 0.21875
- m_gain: float32 [768], replicated, may hold values from 0.1 to 1.9
- m_up: bfloat16 [768, 3072], P(None, 'heads'), may hold values from -0.21875 to 0.21875
- m_down: bfloat16 [3072, 768], P('heads'), may hold values from -0.109375 to 0.109375
- m_merge: bfloat16 [3, 768, 768], replicated, may hold values from -0.125 to 0.125
Outputs:
- block_out: bfloat16 [128, 196, 768], P('tm', 'heads')
- merged: bfloat16 [64, 196, 768], P('tm', 'heads')
All inputs are finite; a program needn't handle non-finite values.
Results may differ from a plain program's by a relative error of at most 0.02.
Values may be sent and summed in bfloat16 or wider, within the bound.
A program may use at most 64 MiB of HBM per device.

v0:
```python
import jax
import jax.numpy as jnp
from jax import lax
from jax.sharding import PartitionSpec as P

HD = 64


def shifted(block, axis, distance):
    devices = range(lax.axis_size(axis))
    route = [(i - distance, i) for i in devices if i - distance in devices]
    return lax.ppermute(block, axis, route)


def layer_norm(values, gain):
    floats = values.astype(jnp.float32)
    centre = jnp.mean(floats, axis=-1, keepdims=True)
    spread = jnp.mean((floats - centre) ** 2, axis=-1, keepdims=True)
    return (floats - centre) * lax.rsqrt(spread + 1e-06) * gain


def project(rows, matrix):
    product = lax.dot_general(
        rows, matrix, (((1,), (1,)), ((), ())), preferred_element_type=jnp.float32
    )
    return product.astype(jnp.bfloat16)


def local(video, t_gain, t_qkv, t_out, s_gain, s_qkv, s_out, m_gain, m_up, m_down, m_merge):
    tm_count = lax.axis_size("tm")
    head_count = lax.axis_size("heads")
    head_index = lax.axis_index("heads")
    frames, positions, model_width = video.shape
    local_width = t_qkv.shape[1]
    head_size = HD
    local_heads = local_width // head_size
    scale_factor = head_size ** (-0.5)
    padded_count = -(-positions // tm_count) * tm_count
    position_share = positions // head_count
    position_start = head_index * position_share

    def own_positions(values):
        return lax.dynamic_slice_in_dim(values, position_start, position_share, 1)

    normed = layer_norm(video, t_gain).astype(jnp.bfloat16).reshape(-1, model_width)
    query_rows = project(normed, t_qkv[0]).reshape(frames, positions, local_heads, head_size)
    key_rows = project(normed, t_qkv[1]).reshape(frames, positions, local_heads, head_size)
    value_rows = project(normed, t_qkv[2]).reshape(frames, positions, local_heads, head_size)
    stacked = jnp.concatenate([query_rows, key_rows, value_rows], axis=3)
    stacked = jnp.pad(stacked, ((0, 0), (0, padded_count - positions), (0, 0), (0, 0)))
    stacked = stacked.reshape(frames, padded_count * local_heads, 3 * head_size)
    exchanged = lax.all_to_all(stacked, "tm", split_axis=1, concat_axis=0, tiled=True)
    item_queries = exchanged[:, :, :head_size]
    item_keys = exchanged[:, :, head_size : 2 * head_size]
    item_values = exchanged[:, :, 2 * head_size :]
    scores = (
        jnp.einsum("fid,gid->ifg", item_queries, item_keys, preferred_element_type=jnp.float32)
        * scale_factor
    )
    weights = jax.nn.softmax(scores, axis=-1).astype(jnp.bfloat16)
    mixed = jnp.einsum(
        "ifg,gid->fid", weights, item_values, preferred_element_type=jnp.float32
    ).astype(jnp.bfloat16)
    returned = lax.all_to_all(mixed, "tm", split_axis=0, concat_axis=1, tiled=True)
    mixed_rows = returned[:, : positions * local_heads].reshape(frames * positions, local_width)
    partial_value = jnp.dot(mixed_rows, t_out, preferred_element_type=jnp.float32).reshape(
        frames, positions, model_width
    )
    summed = lax.psum_scatter(
        partial_value.astype(jnp.bfloat16), "heads", scatter_dimension=1, tiled=True
    ).astype(jnp.float32)
    time_part = (own_positions(video).astype(jnp.float32) + summed).astype(jnp.bfloat16)
    after_time = lax.all_gather(time_part, "heads", axis=1, tiled=True)
    normed = layer_norm(after_time, s_gain).astype(jnp.bfloat16).reshape(-1, model_width)
    query_rows = project(normed, s_qkv[0]).reshape(frames, positions, local_heads, head_size)
    key_rows = project(normed, s_qkv[1]).reshape(frames, positions, local_heads, head_size)
    value_rows = project(normed, s_qkv[2]).reshape(frames, positions, local_heads, head_size)
    scores = (
        jnp.einsum("fphd,frhd->fhpr", query_rows, key_rows, preferred_element_type=jnp.float32)
        * scale_factor
    )
    weights = jax.nn.softmax(scores, axis=-1).astype(jnp.bfloat16)
    mixed = jnp.einsum(
        "fhpr,frhd->fphd", weights, value_rows, preferred_element_type=jnp.float32
    ).astype(jnp.bfloat16)
    partial_value = jnp.dot(
        mixed.reshape(-1, local_width), s_out, preferred_element_type=jnp.float32
    ).reshape(frames, positions, model_width)
    summed = lax.psum_scatter(
        partial_value.astype(jnp.bfloat16), "heads", scatter_dimension=1, tiled=True
    ).astype(jnp.float32)
    space_part = (own_positions(after_time).astype(jnp.float32) + summed).astype(jnp.bfloat16)
    after_space = lax.all_gather(space_part, "heads", axis=1, tiled=True)
    normed = layer_norm(after_space, m_gain).astype(jnp.bfloat16).reshape(-1, model_width)
    hidden = jax.nn.gelu(
        jnp.dot(normed, m_up, preferred_element_type=jnp.float32), approximate=False
    ).astype(jnp.bfloat16)
    partial_value = jnp.dot(hidden, m_down, preferred_element_type=jnp.float32).reshape(
        frames, positions, model_width
    )
    summed = lax.psum_scatter(
        partial_value.astype(jnp.bfloat16), "heads", scatter_dimension=1, tiled=True
    ).astype(jnp.float32)
    block_out = (space_part.astype(jnp.float32) + summed).astype(jnp.bfloat16)
    edge_rows = shifted(block_out[frames - 1], "tm", 1)
    extended = jnp.concatenate([edge_rows[None], block_out], axis=0)
    merge_sum = jnp.zeros((frames // 2 * position_share, model_width), jnp.float32)
    for offset in range(3):
        picked = extended[offset : offset + frames : 2].reshape(
            frames // 2 * position_share, model_width
        )
        merge_sum = merge_sum + jnp.dot(picked, m_merge[offset], preferred_element_type=jnp.float32)
    merged = merge_sum.reshape(frames // 2, position_share, model_width).astype(jnp.bfloat16)
    return (block_out, merged)


def solution(mesh):
    placed = (
        P("tm", None, None),
        P(),
        P(None, "heads", None),
        P("heads", None),
        P(),
        P(None, "heads", None),
        P("heads", None),
        P(),
        P(None, "heads"),
        P("heads", None),
        P(),
    )
    return jax.shard_map(
        local,
        mesh=mesh,
        in_specs=placed,
        out_specs=(P("tm", "heads", None), P("tm", "heads", None)),
        check_vma=False,
    )
```

profile of v0, /device:TPU:1, one launch (start us, length us, event | category | flops | bytes accessed | tf_op | source)
XLA Modules:
  0.0 290.6 jit_solution(796264900034656760)
XLA Ops:
  7.2 1.7 convert_reduce_fusion.2
  9.0 1.2 fusion.21
  10.2 1.0 fusion.23
  11.3 0.1 reshape.95
  11.5 1.4 convolution_convert_fusion.8
  12.9 0.4 convolution_convert_fusion.9
  13.3 0.4 convolution_convert_fusion.10
  13.7 0.2 reshape.98
  13.8 0.9 copy.69
  14.8 0.2 reshape.96
  14.9 0.2 reshape.97
  15.1 0.9 copy.68
  16.0 0.9 copy.67
  17.0 4.1 %fusion.57 = bf16[2,256,3,192]{3,0,2,1:T(2,128)(2,1)S(1)} fusion(bf16[2,196,3,64]{3,0,2,1:T(2,128)(2,1)S(1)} %copy.69, bf16[2,196,3,64]{3,0,2,1:T(2,128)(2,1)S(1)} %copy.68, bf16[2,196,3,64]{3,0,2,1:T(2,128)(2,1)S(1)} %copy.67), kind=kLoop, calls=%fused_computation.79 | loop fusion | flops 2949120 | bytes 1041408 | tf_op jit(solution)/shard_map/concatenate | solution.py:49
  21.1 35.7 %all_to_all.36 = bf16[2,768,192]{2,0,1:T(2,128)(2,1)S(1)} all-to-all(bf16[2,768,192]{2,0,1:T(2,128)(2,1)S(1)} %bitcast.90), channel_id=1, replica_groups=mesh['tm'=64,'heads'=4] {'tm'}, dimensions={1} | all-to-all | bytes 1179648 | tf_op jit(solution)/shard_map/all_to_all | solution.py:52
  56.8 0.7 copy.70
  57.4 0.7 all_to_all.29
  58.2 1.1 fusion.156
  59.3 0.4 convolution_multiply_fusion.1
  59.7 1.1 fusion.43
  60.8 0.4 copy.75
  61.2 0.3 reshape.111
  61.5 18.1 %all_to_all.37 = bf16[64,2,768]{2,1,0:T(2,128)(2,1)S(1)} all-to-all(bf16[64,2,768]{2,1,0:T(2,128)(2,1)S(1)} %reshape.111), channel_id=1, replica_groups=mesh['tm'=64,'heads'=4] {'tm'}, dimensions={0} | all-to-all | bytes 393216 | tf_op jit(solution)/shard_map/all_to_all | solution.py:64
  79.6 0.3 reshape.112
  80.0 0.3 copy.77
  80.3 0.2 slice.68
  80.6 0.3 dot_general.60
  81.0 0.3 convolution_convert_fusion.1
  81.3 1.3 copy.80
  82.7 0.6 dynamic-slice
  83.9 40.4 %all-reduce.8.cloned.1.call-done = bf16[2,196,768]{2,0,1:T(2,128)(2,1)} async-done(((bf16[2,196,768]{2,0,1:T(2,128)(2,1)}), bf16[2,196,768]{2,0,1:T(2,128)(2,1)}) %all-reduce.8.cloned.1.call-update) | async-done | bytes 602128
  124.3 1.1 add_convert_fusion.2
  125.4 10.5 %all_gather.6 = bf16[2,196,768]{2,0,1:T(2,128)(2,1)S(1)} all-gather(bf16[2,49,768]{2,0,1:T(2,128)(2,1)S(1)} %add_convert_fusion.2), channel_id=1, replica_groups=mesh['tm'=64,'heads'=4] {'heads'}, dimensions={1}, use_global_device_ids=true | all-gather | bytes 752640 | tf_op jit(solution)/shard_map/all_gather | solution.py:73
  135.9 0.5 convert_reduce_fusion.1
  136.5 1.2 fusion.18
  137.7 1.0 fusion.20
  138.8 0.1 reshape.100
  138.9 1.4 convolution_convert_fusion.5
  140.4 0.4 convolution_convert_fusion.6
  140.8 0.4 convolution_convert_fusion.7
  141.1 0.2 reshape.103
  141.3 0.2 reshape.101
  141.4 0.2 reshape.102
  141.6 1.6 fusion.161
  143.2 1.6 convolution_convert_fusion.3
  144.8 0.4 convolution_convert_fusion
  145.2 1.3 copy.87
  146.7 51.5 %all-reduce.10.cloned.1.call-done = bf16[2,196,768]{2,0,1:T(2,128)(2,1)} async-done(((bf16[2,196,768]{2,0,1:T(2,128)(2,1)}), bf16[2,196,768]{2,0,1:T(2,128)(2,1)}) %all-reduce.10.cloned.1.call-update) | async-done | bytes 602128
  198.1 1.0 constant_dynamic-slice_fusion.1
  199.3 10.7 %all_gather.7 = bf16[2,196,768]{2,0,1:T(2,128)(2,1)S(1)} all-gather(bf16[2,49,768]{2,0,1:T(2,128)(2,1)S(1)} %copy.89), channel_id=1, replica_groups=mesh['tm'=64,'heads'=4] {'heads'}, dimensions={1}, use_global_device_ids=true | all-gather | bytes 752640 | tf_op jit(solution)/shard_map/all_gather | solution.py:93
  210.0 0.5 convert_reduce_fusion
  210.5 1.2 fusion.15
  211.7 1.0 fusion.17
  212.8 0.1 reshape.104
  213.0 4.8 %convolution_convert_fusion.2 = bf16[392,768]{1,0:T(8,128)(2,1)S(1)} fusion(bf16[768,768]{1,0:T(8,128)(2,1)S(1)} %copy-done, bf16[392,768]{1,0:T(8,128)(2,1)S(1)} %reshape.104, bf16[768,768]{1,0:T(8,128)(2,1)} %param.19), kind=kOutput, calls=%fused_computation.19 | convolution fusion | flops 944713728 | bytes 3563520 | tf_op jit(solution)/shard_map/dot_general | solution.py:98
  217.8 0.1 convert_element_type.133
  217.9 1.3 copy.91
  219.2 51.7 %all-reduce.12.cloned.1.call-done = bf16[2,196,768]{2,0,1:T(2,128)(2,1)} async-done(((bf16[2,196,768]{2,0,1:T(2,128)(2,1)}), bf16[2,196,768]{2,0,1:T(2,128)(2,1)}) %all-reduce.12.cloned.1.call-update) | async-done | bytes 602128
  270.9 1.0 constant_dynamic-slice_fusion
  272.0 5.8 %collective-permute-start = (bf16[49,768]{1,0:T(8,128)(2,1)S(1)}, bf16[49,768]{1,0:T(8,128)(2,1)S(1)}, u32[]{:S(2)}, u32[]{:S(2)}) collective-permute-start(bf16[49,768]{1,0:T(8,128)(2,1)S(1)} %slice_bitcast_fusion.2), channel_id=1, source_target_pairs={{0,4},{4,8},{8,12},{12,16},{16,20},{20,24},{24,28},{28,32},{32,36}... | collective-permute-start | bytes 225800 | tf_op jit(solution)/shard_map/ppermute | solution.py:12
  277.8 1.6 fusion.34
  279.4 1.6 fusion.36
  281.0 0.8 copy.93
  281.8 2.2 fusion.53
  (43 shorter events, 1.1 us)
Async XLA Ops:
  7.2 205.8 %copy-start = (bf16[768,768]{1,0:T(8,128)(2,1)S(1)}, bf16[768,768]{1,0:T(8,128)(2,1)}, u32[]{:S(2)}) copy-start(bf16[768,768]{1,0:T(8,128)(2,1)} %param.20) | copy-start | bytes 3538948
  7.2 1.8 copy-start.1
  7.2 3.0 %copy-start.4 = (f32[768]{0:T(1024)S(1)}, f32[768]{0:T(1024)}, u32[]{:S(2)}) copy-start(f32[768]{0:T(1024)} %param.12) | copy-start | bytes 9220
  7.2 117.1 %all-reduce.8.cloned.1.call-start = ((), (), s32[]{:S(2)}) async-start(), calls=%async_computation.2 | async-start | bytes 1204224
  11.4 1.4 copy-start.7
  80.0 1.0 copy-start.2
  81.3 1.4 copy-start.9
  82.6 115.5 %all-reduce.10.cloned.1.call-start = ((), (), s32[]{:S(2)}) async-start(), calls=%async_computation.3 | async-start | bytes 1204224
  125.4 12.3 %copy-start.5 = (f32[768]{0:T(1024)S(1)}, f32[768]{0:T(1024)}, u32[]{:S(2)}) copy-start(f32[768]{0:T(1024)} %param.15) | copy-start | bytes 9220
  138.9 1.4 copy-start.8
  143.2 1.6 copy-start.3
  146.5 124.5 %all-reduce.12.cloned.1.call-start = ((), (), s32[]{:S(2)}) async-start(), calls=%async_computation.4 | async-start | bytes 1204224
  199.3 12.4 %copy-start.6 = (f32[768]{0:T(1024)S(1)}, f32[768]{0:T(1024)}, u32[]{:S(2)}) copy-start(f32[768]{0:T(1024)} %param.18) | copy-start | bytes 9220
  272.0 9.8 %collective-permute-start = (bf16[49,768]{1,0:T(8,128)(2,1)S(1)}, bf16[49,768]{1,0:T(8,128)(2,1)S(1)}, u32[]{:S(2)}, u32[]{:S(2)}) collective-permute-start(bf16[49,768]{1,0:T(8,128)(2,1)S(1)} %slice_bitcast_fusion.2), channel_id=1, source_target_pairs={{0,4},{4,8},{8,12},{12,16},{16,20},{20,24},{24,28},{28,32},{32,36}... | collective-permute-start | bytes 225800 | tf_op jit(solution)/shard_map/ppermute | solution.py:12
Sparse Core Ops, SparseCore 0:
  82.7 41.5 all-reduce.7
  146.6 51.4 all-reduce.9
  219.3 51.5 all-reduce.11
where the time goes:
time: 291 us
  waiting for transfers between devices  144 us (49%)
  blocking collectives  74.9 us (26%)
  matrix products  21 us (7%)
  local copies, waits for them, and re-layouts  15.4 us (5%)
  between operations  15 us (5%)
  other arithmetic  14.7 us (5%)
  starting transfers between devices  5.93 us (2%)
    unnamed x6, waiting for transfers between devices  144 us
    all_to_all x1, blocking collectives, local(): lax.all_to_all(stacked, 'tm', split_axis=1, concat_axis=0, tiled=True)  35.7 us
    all_to_all x1, blocking collectives, local(): lax.all_to_all(mixed, 'tm', split_axis=0, concat_axis=1, tiled=True)  18.1 us
    all_gather x1, blocking collectives, local(): after_space = lax.all_gather(space_part, 'heads', axis=1, tiled=True)  10.7 us
    all_gather x1, blocking collectives, local(): after_time = lax.all_gather(time_part, 'heads', axis=1, tiled=True)  10.5 us
  transfers between devices with their start and end apart: 4, of which 3 were waited for; matrix products, arithmetic and copies ran while one was open for 2% of the time, Pallas kernels for 0%

commit v1 on v0

v1 whole, which is shorter than its diff:
```python
import jax
import jax.numpy as jnp
from jax import lax
from jax.experimental import pallas as pl
from jax.experimental.pallas import tpu as pltpu
from jax.sharding import PartitionSpec as P

HD = 64
MESH = pl.DeviceIdType.MESH
F32 = jnp.float32
BF16 = jnp.bfloat16


def layer_norm(floats, gain):
    centre = jnp.mean(floats, axis=-1, keepdims=True)
    moved = floats - centre
    spread = jnp.mean(moved * moved, axis=-1, keepdims=True)
    return (moved * lax.rsqrt(spread + 1e-06) * gain).astype(BF16)


def dot(a, b):
    return jnp.dot(a, b, preferred_element_type=F32)


def dot_t(a, b):
    return lax.dot_general(a, b, (((1,), (1,)), ((), ())), preferred_element_type=F32)


def iota(shape, axis):
    return lax.broadcasted_iota(jnp.int32, shape, axis)


def attend(queries, keys, values, valid):
    scores = dot_t(queries, keys) * (HD ** -0.5)
    if valid is not None:
        scores = jnp.where(valid, scores, -jnp.inf)
    raised = jnp.exp(scores - jnp.max(scores, axis=-1, keepdims=True))
    total = jnp.sum(raised, axis=-1, keepdims=True)
    return dot(raised.astype(BF16), values) / total


def kernel(
    video, t_gain, t_qkv, t_out, s_gain, s_qkv, s_out, m_gain, m_up, m_down, m_merge,
    block_out, merged,
    vid, w_tqkv, w_tout, w_sqkv, w_sout, w_up, w_down, w_merge,
    fsend, frecv, frecv_extra, rsend, rsend_extra, rrecv,
    hbuf, sqkv, smix, mix_send, mix_recv, gbuf, psend, precv, edge_send, edge_recv,
    load_sem, wt_send, wt_recv, ws_send, ws_recv,
    f_sem, r_sem, h_send, h_recv, x_send, x_recv, g_send, g_recv, p_send, p_recv, e_sem,
):
    tm = lax.axis_index("tm")
    hx = lax.axis_index("heads")
    count = lax.axis_size("tm")
    wide = lax.axis_size("heads")
    positions, model = video.shape[1], video.shape[2]
    quarter = positions // wide
    group = count // wide
    width = t_qkv.shape[1]
    heads = width // HD
    home = tm // group
    rank = lax.rem(tm, group)
    last = rank == group - 1
    rows = hbuf.shape[1]
    half = rows // 2

    def peer(step):
        return lax.rem(hx + step, wide)

    loads = []
    for i, (source, target) in enumerate(
        (
            (video, vid), (t_qkv, w_tqkv), (t_out, w_tout.at[hx]), (s_qkv, w_sqkv),
            (s_out, w_sout.at[hx]), (m_up, w_up), (m_down, w_down), (m_merge, w_merge),
        )
    ):
        copy = pltpu.make_async_copy(source, target, load_sem.at[i])
        copy.start()
        loads.append(copy)

    barrier = pltpu.get_barrier_semaphore()

    @pl.loop(1, count)
    def _(step):
        pl.semaphore_signal(
            barrier, inc=1, device_id={"tm": lax.rem(tm + step, count)}, device_id_type=MESH
        )

    for step in range(1, wide):
        pl.semaphore_signal(
            barrier, inc=1, device_id={"heads": peer(step)}, device_id_type=MESH
        )

    loads[0].wait()
    loads[1].wait()
    tqkv = w_tqkv[...].reshape(3 * width, model)
    for f in range(2):
        normed = layer_norm(vid[f].astype(F32), t_gain[...])
        fsend[:, f] = dot_t(normed, tqkv).astype(BF16)

    pl.semaphore_wait(barrier, count - 1 + wide - 1)

    def first_position(device):
        return (device // group) * quarter + lax.rem(device, group) * 3

    @pl.loop(1, count)
    def _(step):
        to = lax.rem(tm + step, count)
        start = first_position(to)
        pltpu.make_async_remote_copy(
            fsend.at[pl.ds(start, 3)], frecv.at[tm], f_sem.at[0], f_sem.at[1],
            device_id={"tm": to}, device_id_type=MESH,
        ).start()

        @pl.when(lax.rem(to, group) == group - 1)
        def _():
            pltpu.make_async_remote_copy(
                fsend.at[start + 3], frecv_extra.at[tm], f_sem.at[2], f_sem.at[3],
                device_id={"tm": to}, device_id_type=MESH,
            ).start()

    own_start = first_position(tm)
    pltpu.make_async_copy(fsend.at[pl.ds(own_start, 3)], frecv.at[tm], f_sem.at[1]).start()

    @pl.when(last)
    def _():
        pltpu.make_async_copy(fsend.at[own_start + 3], frecv_extra.at[tm], f_sem.at[3]).start()

    gathers = []
    for source, target, send, recv in (
        (t_out, w_tout, wt_send, wt_recv), (s_out, w_sout, ws_send, ws_recv),
    ):
        copies = []
        for step in (1, 3, 2):
            copy = pltpu.make_async_remote_copy(
                source, target.at[hx], send.at[step], recv.at[step],
                device_id={"heads": peer(step)}, device_id_type=MESH,
            )
            copy.start()
            copies.append(copy)
        gathers.append(copies)

    row = iota((rows, positions), 0)
    column = iota((rows, positions), 1)
    place = lax.rem(row, half)
    own_video = jnp.zeros((rows, model), F32)
    for f in range(2):
        pick = (row // half == f) & (place < quarter) & (column == hx * quarter + place)
        own_video += dot(pick.astype(BF16), vid[f])

    pltpu.make_async_copy(frecv, frecv, f_sem.at[1]).wait()

    def temporal(block):
        parts = []
        for head in range(heads):
            at = head * HD
            parts.append(
                attend(
                    block[:, at : at + HD],
                    block[:, width + at : width + at + HD],
                    block[:, 2 * width + at : 2 * width + at + HD],
                    None,
                )
            )
        mixed = jnp.concatenate(parts, axis=1).astype(BF16)
        return mixed.reshape(count, 2, width)

    for p in range(3):
        rsend[:, p] = temporal(frecv[:, p].reshape(2 * count, 3 * width))

    @pl.when(last)
    def _():
        pltpu.make_async_copy(frecv_extra, frecv_extra, f_sem.at[3]).wait()
        rsend_extra[...] = temporal(frecv_extra[...].reshape(2 * count, 3 * width))

    def send_back(to, local):
        pieces = [(rsend.at[to], rrecv.at[hx, pl.ds(3 * rank, 3)], 0, 1)]
        extra = (rsend_extra.at[to], rrecv.at[hx, 3 * group], 2, 3)

        def go(source, target, send, recv):
            if local:
                pltpu.make_async_copy(source, target, r_sem.at[recv]).start()
            else:
                pltpu.make_async_remote_copy(
                    source, target, r_sem.at[send], r_sem.at[recv],
                    device_id={"tm": to, "heads": home}, device_id_type=MESH,
                ).start()

        go(*pieces[0])

        @pl.when(last)
        def _():
            go(*extra)

    @pl.loop(1, count)
    def _(step):
        send_back(lax.rem(tm + step, count), False)

    @pl.when(home == hx)
    def _():
        send_back(tm, True)

    @pl.when(home != hx)
    def _():
        send_back(tm, False)

    pltpu.make_async_copy(
        fsend.at[pl.ds(0, 3 * (count - 1))], fsend.at[pl.ds(0, 3 * (count - 1))], f_sem.at[0]
    ).wait()

    @pl.when(last)
    def _():
        part = fsend.at[pl.ds(0, wide - 1)]
        pltpu.make_async_copy(part, part, f_sem.at[2]).wait()

    @pl.when(jnp.logical_not(last))
    def _():
        part = fsend.at[pl.ds(0, wide)]
        pltpu.make_async_copy(part, part, f_sem.at[2]).wait()

    loads[2].wait()
    for copy in gathers[0]:
        copy.wait()
    row = iota((rows, 2 * quarter), 0)
    column = iota((rows, 2 * quarter), 1)
    place = lax.rem(row, half)
    order = ((place < quarter) & (column == 2 * place + row // half)).astype(BF16)

    most = rrecv.at[:, pl.ds(0, 3 * group)]
    pltpu.make_async_copy(most, most, r_sem.at[1]).wait()
    rest = rrecv.at[:, 3 * group]
    pltpu.make_async_copy(rest, rest, r_sem.at[3]).wait()
    total = own_video
    for x in range(wide):
        mixed = dot(order, rrecv[x].reshape(2 * quarter, width)).astype(BF16)
        total += dot(mixed, w_tout[x])
    x1 = total.astype(BF16).astype(F32)

    def gather(buffer, send, recv):
        copies = {}
        for step in (1, 3, 2):
            copies[step] = pltpu.make_async_remote_copy(
                buffer.at[hx], buffer.at[hx], send.at[step], recv.at[step],
                device_id={"heads": peer(step)}, device_id_type=MESH,
            )
            copies[step].start()
        return copies

    hbuf[hx] = layer_norm(x1, s_gain[...])
    copies = gather(hbuf, h_send, h_recv)
    loads[3].wait()
    for step in (0, 1, 3, 2):
        if step:
            copies[step].wait_recv()
        at = peer(wide - step)
        projected = dot_t(hbuf[at], w_sqkv[...].reshape(3 * width, model))
        for f in range(2):
            sqkv[f, at] = projected[f * half : (f + 1) * half]
    keep = lax.rem(iota((1, wide * half), 1), half) < quarter
    for f in range(2):
        block = sqkv[f].reshape(wide * half, 3 * width).astype(BF16)
        for head in range(heads):
            at = head * HD
            smix[:, f, :, at : at + HD] = attend(
                block[:, at : at + HD],
                block[:, width + at : width + at + HD],
                block[:, 2 * width + at : 2 * width + at + HD],
                keep,
            ).reshape(wide, half, HD)
    mix_send[...] = smix[...].reshape(wide, rows, width).astype(BF16)
    mix_copies = []
    for step in (2, 1, 3):
        copy = pltpu.make_async_remote_copy(
            mix_send.at[peer(step)], mix_recv.at[hx], x_send.at[step], x_recv.at[step],
            device_id={"heads": peer(step)}, device_id_type=MESH,
        )
        copy.start()
        mix_copies.append(copy)
    loads[4].wait()
    for copy in gathers[1]:
        copy.wait()
    total = x1 + dot(mix_send[hx], w_sout[hx])
    for step, copy in zip((2, 1, 3), mix_copies):
        copy.wait_recv()
        at = peer(wide - step)
        total += dot(mix_recv[at], w_sout[at])
    x2 = total.astype(BF16).astype(F32)

    gbuf[hx] = layer_norm(x2, m_gain[...])
    g_copies = gather(gbuf, g_send, g_recv)
    loads[5].wait()
    loads[6].wait()
    p_copies = []
    own_part = None
    for step in (0, 1, 3, 2):
        if step:
            g_copies[step].wait_recv()
        at = peer(wide - step)
        up = dot(gbuf[at], w_up[...])
        hidden = (0.5 * up * (1.0 + lax.erf(up * (0.5 ** 0.5)))).astype(BF16)
        part = dot(hidden, w_down[...])
        if step:
            psend[at] = part.astype(BF16)
            copy = pltpu.make_async_remote_copy(
                psend.at[at], precv.at[hx], p_send.at[step], p_recv.at[step],
                device_id={"heads": at}, device_id_type=MESH,
            )
            copy.start()
            p_copies.append((step, copy))
        else:
            own_part = part
    total = x2 + own_part
    for step, copy in p_copies:
        copy.wait_recv()
        total += precv[peer(step)].astype(F32)
    for f in range(2):
        block_out[f] = total[f * half : f * half + quarter].astype(BF16)
    first = total[:half].astype(BF16)
    second = total[half:].astype(BF16)

    edge_send[0:half] = second
    edge_send[half:] = jnp.zeros((edge_send.shape[0] - half, model), BF16)
    to_next = pltpu.make_async_remote_copy(
        edge_send, edge_recv, e_sem.at[0], e_sem.at[1],
        device_id={"tm": lax.rem(tm + 1, count)}, device_id_type=MESH,
    )

    @pl.when(tm < count - 1)
    def _():
        to_next.start()

    loads[7].wait()
    result = dot(first, w_merge[1]) + dot(second, w_merge[2])

    @pl.when(tm > 0)
    def _():
        to_next.wait_recv()

    @pl.when(tm == 0)
    def _():
        edge_recv[...] = jnp.zeros_like(edge_recv)

    result += dot(edge_recv[0:half], w_merge[0])
    merged[0] = result[:quarter].astype(BF16)

    @pl.when(tm < count - 1)
    def _():
        to_next.wait_send()

    @pl.when(home == hx)
    def _():
        part = rsend.at[pl.ds(0, count - 1)]
        pltpu.make_async_copy(part, part, r_sem.at[0]).wait()

        @pl.when(last)
        def _():
            part = rsend_extra.at[pl.ds(0, count - 1)]
            pltpu.make_async_copy(part, part, r_sem.at[2]).wait()

    @pl.when(home != hx)
    def _():
        pltpu.make_async_copy(rsend, rsend, r_sem.at[0]).wait()

        @pl.when(last)
        def _():
            pltpu.make_async_copy(rsend_extra, rsend_extra, r_sem.at[2]).wait()

    for step in (1, 2, 3):
        copies[step].wait_send()
        g_copies[step].wait_send()
    for copy in mix_copies:
        copy.wait_send()
    for _, copy in p_copies:
        copy.wait_send()


def local(video, t_gain, t_qkv, t_out, s_gain, s_qkv, s_out, m_gain, m_up, m_down, m_merge):
    count = lax.axis_size("tm")
    wide = lax.axis_size("heads")
    frames, positions, model = video.shape
    width = t_qkv.shape[1]
    hidden = m_up.shape[1]
    quarter = positions // wide
    half = -(-quarter // 8) * 8
    rows = 2 * half
    edge = -(-half // 16) * 16
    vmem = pltpu.VMEM
    dma = pltpu.SemaphoreType.DMA
    in_vmem = pl.BlockSpec(memory_space=pltpu.VMEM)
    anywhere = pl.BlockSpec(memory_space=pl.ANY)
    return pl.pallas_call(
        kernel,
        out_shape=(
            jax.ShapeDtypeStruct((frames, quarter, model), BF16),
            jax.ShapeDtypeStruct((frames // 2, quarter, model), BF16),
        ),
        in_specs=[
            anywhere, in_vmem, anywhere, anywhere, in_vmem, anywhere, anywhere, in_vmem,
            anywhere, anywhere, anywhere,
        ],
        out_specs=(in_vmem, in_vmem),
        scratch_shapes=[
            vmem((frames, positions, model), BF16),
            vmem((3, width, model), BF16),
            vmem((wide, width, model), BF16),
            vmem((3, width, model), BF16),
            vmem((wide, width, model), BF16),
            vmem((model, hidden), BF16),
            vmem((hidden, model), BF16),
            vmem((3, model, model), BF16),
            vmem((positions, 2, 3 * width), BF16),
            vmem((count, 3, 2, 3 * width), BF16),
            vmem((count, 2, 3 * width), BF16),
            vmem((count, 3, 2, width), BF16),
            vmem((count, 2, width), BF16),
            vmem((wide, quarter, 2, width), BF16),
            vmem((wide, rows, model), BF16),
            vmem((2, wide, half, 3 * width), F32),
            vmem((wide, 2, half, width), F32),
            vmem((wide, rows, width), BF16),
            vmem((wide, rows, width), BF16),
            vmem((wide, rows, model), BF16),
            vmem((wide, rows, model), BF16),
            vmem((wide, rows, model), BF16),
            vmem((edge, model), BF16),
            vmem((edge, model), BF16),
            dma((8,)), dma((4,)), dma((4,)), dma((4,)), dma((4,)),
            dma((4,)), dma((4,)), dma((4,)), dma((4,)), dma((4,)), dma((4,)),
            dma((4,)), dma((4,)), dma((4,)), dma((4,)), dma((2,)),
        ],
        compiler_params=pltpu.CompilerParams(
            collective_id=0, has_side_effects=True, vmem_limit_bytes=50 * 2**20
        ),
    )(
        video, t_gain[None], t_qkv, t_out, s_gain[None], s_qkv, s_out, m_gain[None],
        m_up, m_down, m_merge,
    )


def solution(mesh):
    placed = (
        P("tm", None, None),
        P(),
        P(None, "heads", None),
        P("heads", None),
        P(),
        P(None, "heads", None),
        P("heads", None),
        P(),
        P(None, "heads"),
        P("heads", None),
        P(),
    )
    return jax.shard_map(
        local,
        mesh=mesh,
        in_specs=placed,
        out_specs=(P("tm", "heads", None), P("tm", "heads", None)),
        check_vma=False,
    )
```

time: 291 us -> 90.6 us (0.31)
  waiting for transfers between devices: 144 us -> 0 us
  Pallas kernels: 0 us -> 82.8 us
  blocking collectives: 74.9 us -> 0 us
  matrix products: 21 us -> 0 us
  other arithmetic: 14.7 us -> 0 us
  between operations: 15 us -> 0.68 us
  local copies, waits for them, and re-layouts: 15.4 us -> 6.84 us
  starting transfers between devices: 5.93 us -> 0 us
    unnamed x6 -> x0, waiting for transfers between devices: 144 us -> none
    pallas_call x0 -> x1, Pallas kernels: none -> 82.8 us  [local(): pl.pallas_call(kernel, out_shape=(jax.ShapeDtypeStruct((frames, quarter,...]
    all_to_all x2 -> x0, blocking collectives: 53.8 us -> none  [the longest x1 35.7 us: local(): lax.all_to_all(stacked, 'tm', split_axis=1, concat_axis=0, tiled=True)]
    all_gather x2 -> x0, blocking collectives: 21.2 us -> none  [the longest x1 10.7 us: local(): after_space = lax.all_gather(space_part, 'heads', axis=1, tiled=True)]
    dot_general x15 -> x0, matrix products: 18.3 us -> none  [the longest x3 5.45 us: local(): jnp.dot(picked, m_merge[offset], preferred_element_type=jnp.float32)]
    reduce_sum x6 -> x0, other arithmetic: 6.27 us -> none  [the longest x3 3.47 us: layer_norm(): spread = jnp.mean((floats - centre) ** 2, axis=-1, keepdims=True)]
    ppermute x1 -> x0, starting transfers between devices: 5.81 us -> none  [shifted(): return lax.ppermute(block, axis, route)]
    convert_element_type x9 -> x0, local copies, waits for them, and re-layouts: 4.7 us -> none  [the longest x4 3.96 us: local(): partial_value.astype(jnp.bfloat16)]
  transfers between devices with their start and end apart: 4 -> 0, of which waited for: 3 -> 0; matrix products, arithmetic and copies ran while one was open for 2% -> 0% of each run, Pallas kernels for 0% -> 0%
where the time goes in v1:
time: 90.6 us; the launch traced here: 90.4 us
  Pallas kernels  82.8 us (91%)
  local copies, waits for them, and re-layouts  6.84 us (8%)
    pallas_call x1, Pallas kernels, local(): pl.pallas_call(kernel, out_shape=(jax.ShapeDtypeStruct((frames, quarter,...  82.8 us
    unnamed x10, local copies, waits for them, and re-layouts  3.9 us

profile of v1, /device:TPU:1, one launch (start us, length us, event | category | flops | bytes accessed | tf_op | source)
XLA Modules:
  0.0 90.4 jit_solution(6507186198066014041)
XLA Ops:
  0.6 0.0 copy-start.2
  0.6 0.0 copy-start
  0.7 0.8 broadcast_in_dim.9.t_gain
  1.4 0.7 broadcast_in_dim.10.s_gain
  2.1 0.7 broadcast_in_dim.11.m_gain
  2.8 1.1 %copy.13.video = bf16[2,196,768]{2,1,0:T(8,128)(2,1)S(1)} copy(bf16[2,196,768]{2,0,1:T(2,128)(2,1)} %param.11) | data formatting | bytes 1204224 | tf_op args[0]
  3.9 0.0 copy-done.2
  4.0 0.0 copy-done
  4.0 0.0 copy-start.1
  4.0 1.2 %copy-done.1 = bf16[3,192,768]{2,1,0:T(8,128)(2,1)S(1)} copy-done((bf16[3,192,768]{2,1,0:T(8,128)(2,1)S(1)}, bf16[3,192,768]{2,1,0:T(8,128)(2,1)}, u32[]{:S(2)}) %copy-start.1) | copy-done | bytes 884760
  5.1 0.0 copy-start.3
  5.1 1.0 %copy-done.3 = bf16[192,768]{1,0:T(8,128)(2,1)S(1)} copy-done((bf16[192,768]{1,0:T(8,128)(2,1)S(1)}, bf16[192,768]{1,0:T(8,128)(2,1)}, u32[]{:S(2)}) %copy-start.3) | copy-done | bytes 294936
  6.1 82.8 %shard_map.122 = (bf16[2,49,768]{2,1,0:T(8,128)(2,1)S(1)}, bf16[1,49,768]{2,1,0:T(8,128)(2,1)S(1)}) custom-call(bf16[2,196,768]{2,1,0:T(8,128)(2,1)S(1)} %copy.13.video, f32[1,768]{1,0:T(1,128)S(1)} %broadcast_in_dim.9.t_gain, bf16[3,192,768]{2,1,0:T(8,128)(2,1)S(1)} %copy-done, bf16[192,768]{1,0:T(8,128)(2,1)S(1)} %copy-done.2, ...), custom_call_target="tpu_custom_call" | custom-call | tf_op jit(solution)/shard_map/pallas_call | solution.py:390
  89.0 0.8 copy.14
  89.7 0.6 copy.16
Async XLA Ops:
  0.6 3.3 %copy-start.2 = (bf16[192,768]{1,0:T(8,128)(2,1)S(1)}, bf16[192,768]{1,0:T(8,128)(2,1)}, u32[]{:S(2)}) copy-start(bf16[192,768]{1,0:T(8,128)(2,1)} %t_out.1) | copy-start | bytes 884740
  0.6 3.3 %copy-start = (bf16[3,192,768]{2,1,0:T(8,128)(2,1)S(1)}, bf16[3,192,768]{2,1,0:T(8,128)(2,1)}, u32[]{:S(2)}) copy-start(bf16[3,192,768]{2,1,0:T(8,128)(2,1)} %t_qkv.1) | copy-start | bytes 2654212
  4.0 1.2 %copy-start.1 = (bf16[3,192,768]{2,1,0:T(8,128)(2,1)S(1)}, bf16[3,192,768]{2,1,0:T(8,128)(2,1)}, u32[]{:S(2)}) copy-start(bf16[3,192,768]{2,1,0:T(8,128)(2,1)} %s_qkv.1) | copy-start | bytes 2654212
  5.1 1.0 %copy-start.3 = (bf16[192,768]{1,0:T(8,128)(2,1)S(1)}, bf16[192,768]{1,0:T(8,128)(2,1)}, u32[]{:S(2)}) copy-start(bf16[192,768]{1,0:T(8,128)(2,1)} %s_out.1) | copy-start | bytes 884740

commit v2 on v1

--- a/solution.py
+++ b/solution.py
@@ -52,7 +52,7 @@
     hx = lax.axis_index("heads")
     count = lax.axis_size("tm")
     wide = lax.axis_size("heads")
-    positions, model = video.shape[1], video.shape[2]
+    positions, model = video.shape[0], video.shape[2]
     quarter = positions // wide
     group = count // wide
     width = t_qkv.shape[1]
@@ -79,11 +79,13 @@
 
     barrier = pltpu.get_barrier_semaphore()
 
-    @pl.loop(1, count)
-    def _(step):
-        pl.semaphore_signal(
-            barrier, inc=1, device_id={"tm": lax.rem(tm + step, count)}, device_id_type=MESH
-        )
+    def other(k):
+        side = lax.rem(k, 2)
+        return lax.rem(tm + count // 2 + (1 - 2 * side) * ((k + side) // 2) + count, count)
+
+    @pl.loop(0, count - 1)
+    def _(k):
+        pl.semaphore_signal(barrier, inc=1, device_id={"tm": other(k)}, device_id_type=MESH)
 
     for step in range(1, wide):
         pl.semaphore_signal(
@@ -93,18 +95,17 @@
     loads[0].wait()
     loads[1].wait()
     tqkv = w_tqkv[...].reshape(3 * width, model)
-    for f in range(2):
-        normed = layer_norm(vid[f].astype(F32), t_gain[...])
-        fsend[:, f] = dot_t(normed, tqkv).astype(BF16)
+    normed = layer_norm(vid[...].reshape(2 * positions, model).astype(F32), t_gain[...])
+    fsend[...] = dot_t(normed, tqkv).astype(BF16).reshape(positions, 2, 3 * width)
 
     pl.semaphore_wait(barrier, count - 1 + wide - 1)
 
     def first_position(device):
         return (device // group) * quarter + lax.rem(device, group) * 3
 
-    @pl.loop(1, count)
-    def _(step):
-        to = lax.rem(tm + step, count)
+    @pl.loop(0, count - 1)
+    def _(k):
+        to = other(k)
         start = first_position(to)
         pltpu.make_async_remote_copy(
             fsend.at[pl.ds(start, 3)], frecv.at[tm], f_sem.at[0], f_sem.at[1],
@@ -139,13 +140,11 @@
             copies.append(copy)
         gathers.append(copies)
 
-    row = iota((rows, positions), 0)
-    column = iota((rows, positions), 1)
+    row = iota((rows, 2 * quarter), 0)
+    column = iota((rows, 2 * quarter), 1)
     place = lax.rem(row, half)
-    own_video = jnp.zeros((rows, model), F32)
-    for f in range(2):
-        pick = (row // half == f) & (place < quarter) & (column == hx * quarter + place)
-        own_video += dot(pick.astype(BF16), vid[f])
+    order = ((place < quarter) & (column == 2 * place + row // half)).astype(BF16)
+    own_video = dot(order, vid[pl.ds(hx * quarter, quarter)].reshape(2 * quarter, model))
 
     pltpu.make_async_copy(frecv, frecv, f_sem.at[1]).wait()
 
@@ -191,9 +190,9 @@
         def _():
             go(*extra)
 
-    @pl.loop(1, count)
-    def _(step):
-        send_back(lax.rem(tm + step, count), False)
+    @pl.loop(0, count - 1)
+    def _(k):
+        send_back(other(k), False)
 
     @pl.when(home == hx)
     def _():
@@ -220,11 +219,6 @@
     loads[2].wait()
     for copy in gathers[0]:
         copy.wait()
-    row = iota((rows, 2 * quarter), 0)
-    column = iota((rows, 2 * quarter), 1)
-    place = lax.rem(row, half)
-    order = ((place < quarter) & (column == 2 * place + row // half)).astype(BF16)
-
     most = rrecv.at[:, pl.ds(0, 3 * group)]
     pltpu.make_async_copy(most, most, r_sem.at[1]).wait()
     rest = rrecv.at[:, 3 * group]
@@ -313,7 +307,7 @@
         copy.wait_recv()
         total += precv[peer(step)].astype(F32)
     for f in range(2):
-        block_out[f] = total[f * half : f * half + quarter].astype(BF16)
+        block_out[:, f] = total[f * half : f * half + quarter].astype(BF16)
     first = total[:half].astype(BF16)
     second = total[half:].astype(BF16)
 
@@ -387,10 +381,10 @@
     dma = pltpu.SemaphoreType.DMA
     in_vmem = pl.BlockSpec(memory_space=pltpu.VMEM)
     anywhere = pl.BlockSpec(memory_space=pl.ANY)
-    return pl.pallas_call(
+    out, together = pl.pallas_call(
         kernel,
         out_shape=(
-            jax.ShapeDtypeStruct((frames, quarter, model), BF16),
+            jax.ShapeDtypeStruct((quarter, frames, model), BF16),
             jax.ShapeDtypeStruct((frames // 2, quarter, model), BF16),
         ),
         in_specs=[
@@ -399,7 +393,7 @@
         ],
         out_specs=(in_vmem, in_vmem),
         scratch_shapes=[
-            vmem((frames, positions, model), BF16),
+            vmem((positions, frames, model), BF16),
             vmem((3, width, model), BF16),
             vmem((wide, width, model), BF16),
             vmem((3, width, model), BF16),
@@ -428,12 +422,13 @@
             dma((4,)), dma((4,)), dma((4,)), dma((4,)), dma((2,)),
         ],
         compiler_params=pltpu.CompilerParams(
-            collective_id=0, has_side_effects=True, vmem_limit_bytes=50 * 2**20
+            collective_id=0, has_side_effects=True, vmem_limit_bytes=60 * 2**20
         ),
     )(
-        video, t_gain[None], t_qkv, t_out, s_gain[None], s_qkv, s_out, m_gain[None],
+        jnp.swapaxes(video, 0, 1), t_gain, t_qkv, t_out, s_gain, s_qkv, s_out, m_gain,
         m_up, m_down, m_merge,
     )
+    return jnp.swapaxes(out, 0, 1), together
 
 
 def solution(mesh):

time: 90.6 us -> 88.1 us (0.972)
  local copies, waits for them, and re-layouts: 6.84 us -> 3.21 us
  Pallas kernels: 82.8 us -> 84.1 us
    broadcast_in_dim x3 -> x0, local copies, waits for them, and re-layouts: 2.16 us -> none  [the longest x1 0.78 us: local(): t_gain[None]]
    pallas_call x1, Pallas kernels: 82.8 us -> 84.1 us  [local(): pl.pallas_call(kernel, out_shape=(jax.ShapeDtypeStruct((quarter, frames,...]
    unnamed x10 -> x2, local copies, waits for them, and re-layouts: 3.9 us -> 3.21 us
where the time goes in v2:
time: 88.1 us; the launch traced here: 88 us
  Pallas kernels  84.1 us (95%)
  local copies, waits for them, and re-layouts  3.21 us (4%)
    pallas_call x1, Pallas kernels, local(): pl.pallas_call(kernel, out_shape=(jax.ShapeDtypeStruct((quarter, frames,...  84.1 us
    unnamed x2, local copies, waits for them, and re-layouts  3.21 us

profile of v2, /device:TPU:1, one launch (start us, length us, event | category | flops | bytes accessed | tf_op | source)
XLA Modules:
  0.0 88.0 jit_solution(6351750348617318488)
XLA Ops:
  0.6 84.1 %shard_map.122 = (bf16[49,2,768]{2,1,0:T(2,128)(2,1)}, bf16[1,49,768]{2,1,0:T(8,128)(2,1)}) custom-call(bf16[196,2,768]{2,1,0:T(2,128)(2,1)} %bitcast.2, f32[768]{0:T(1024)} %t_gain.1, bf16[3,192,768]{2,1,0:T(8,128)(2,1)} %t_qkv.1, bf16[192,768]{1,0:T(8,128)(2,1)} %t_out.1, f32[768]{0:T(1024)} %s_gain.1, bf16[3,192,768]{2,1,0:T(8,128)(2,1)} %s_qkv.1, ...), custom_call_target="tpu_custom_call" | custom-call | tf_op jit(solution)/shard_map/pallas_call | solution.py:384
  84.8 1.7 %copy.15 = bf16[2,49,768]{2,0,1:T(2,128)(2,1)} copy(bf16[2,49,768]{2,0,1:T(2,128)(2,1)} %bitcast.3) | data formatting | bytes 301056
  86.4 1.5 %copy.16 = bf16[1,49,768]{2,1,0:T(8,128)(2,1)} copy(bf16[1,49,768]{2,1,0:T(8,128)(2,1)} %get-tuple-element.9) | data formatting | bytes 150528

commit v3 on v2

--- a/solution.py
+++ b/solution.py
@@ -42,11 +42,10 @@
 def kernel(
     video, t_gain, t_qkv, t_out, s_gain, s_qkv, s_out, m_gain, m_up, m_down, m_merge,
     block_out, merged,
-    vid, w_tqkv, w_tout, w_sqkv, w_sout, w_up, w_down, w_merge,
+    vid, w_tqkv, w_out, w_sqkv, w_mlp, w_merge,
     fsend, frecv, frecv_extra, rsend, rsend_extra, rrecv,
-    hbuf, sqkv, smix, mix_send, mix_recv, gbuf, psend, precv, edge_send, edge_recv,
-    load_sem, wt_send, wt_recv, ws_send, ws_recv,
-    f_sem, r_sem, h_send, h_recv, x_send, x_recv, g_send, g_recv, p_send, p_recv, e_sem,
+    hbuf, sqkv, smix, mix_send, mix_recv, edge_send, edge_recv,
+    load_sem, t_sem, s_sem, w_sem, y_sem, c_sem, f_sem, r_sem, h_sem, x_sem, e_sem,
 ):
     tm = lax.axis_index("tm")
     hx = lax.axis_index("heads")
@@ -63,14 +62,28 @@
     rows = hbuf.shape[1]
     half = rows // 2
 
+    hidden = m_up.shape[1]
+    share = (model + hidden) // 8
+    core = lax.rem(tm, 2)
+    ring = lax.rem(tm // 2, 4)
+
     def peer(step):
         return lax.rem(hx + step, wide)
+
+    def along(step):
+        return tm // 8 * 8 + lax.rem(ring + step, 4) * 2 + core
+
+    def remote(source, target, sems, i, **to):
+        return pltpu.make_async_remote_copy(
+            source, target, sems.at[0, i], sems.at[1, i], device_id=to, device_id_type=MESH
+        )
 
     loads = []
     for i, (source, target) in enumerate(
         (
-            (video, vid), (t_qkv, w_tqkv), (t_out, w_tout.at[hx]), (s_qkv, w_sqkv),
-            (s_out, w_sout.at[hx]), (m_up, w_up), (m_down, w_down), (m_merge, w_merge),
+            (video, vid), (t_qkv, w_tqkv), (m_up, w_mlp.at[0, pl.ds(0, model)]),
+            (m_down, w_mlp.at[0, pl.ds(model, hidden)]), (t_out, w_out.at[0, pl.ds(0, width)]),
+            (s_out, w_out.at[0, pl.ds(width, width)]), (s_qkv, w_sqkv), (m_merge, w_merge),
         )
     ):
         copy = pltpu.make_async_copy(source, target, load_sem.at[i])
@@ -126,19 +139,38 @@
     def _():
         pltpu.make_async_copy(fsend.at[own_start + 3], frecv_extra.at[tm], f_sem.at[3]).start()
 
-    gathers = []
-    for source, target, send, recv in (
-        (t_out, w_tout, wt_send, wt_recv), (s_out, w_sout, ws_send, ws_recv),
-    ):
+    def rows_of(step):
+        return (2 * lax.rem(ring + step, 4) + core) * share
+
+    def piece(step, begin, size):
+        start = pl.multiple_of(rows_of(step) + begin, 16)
+        return w_mlp.at[pl.ds(1, wide - 1), pl.ds(start, size)]
+
+    def fetch(buffer, start, size, sems):
+        start = pl.multiple_of(start, 16)
         copies = []
-        for step in (1, 3, 2):
-            copy = pltpu.make_async_remote_copy(
-                source, target.at[hx], send.at[step], recv.at[step],
-                device_id={"heads": peer(step)}, device_id_type=MESH,
+        for step in (2, 1, 3):
+            copy = remote(
+                buffer.at[0, pl.ds(start, size)], buffer.at[wide - step, pl.ds(start, size)],
+                sems, step, heads=peer(step),
             )
             copy.start()
             copies.append(copy)
-        gathers.append(copies)
+        return copies
+
+    def give(block, i):
+        copy = remote(block, block, c_sem, i, tm=tm + 1 - 2 * core)
+        copy.start()
+        return copy
+
+    half_width = width // 2
+    loads[2].wait()
+    loads[3].wait()
+    w_copies = fetch(w_mlp, rows_of(0), share, w_sem)
+    loads[4].wait()
+    t_copies = fetch(w_out, core * half_width, half_width, t_sem)
+    loads[5].wait()
+    s_copies = fetch(w_out, width + core * half_width, half_width, s_sem)
 
     row = iota((rows, 2 * quarter), 0)
     column = iota((rows, 2 * quarter), 1)
@@ -147,6 +179,19 @@
     own_video = dot(order, vid[pl.ds(hx * quarter, quarter)].reshape(2 * quarter, model))
 
     pltpu.make_async_copy(frecv, frecv, f_sem.at[1]).wait()
+
+    for copy in w_copies:
+        copy.wait_recv()
+    part = share // 2
+    y_copies = [
+        remote(piece(0, 0, part), piece(0, 0, part), y_sem, 0, tm=along(1)),
+        remote(piece(0, part, part), piece(0, part, part), y_sem, 1, tm=along(3)),
+        remote(piece(0, part, part), piece(0, part, part), y_sem, 2, tm=along(1)),
+        remote(piece(0, 0, part), piece(0, 0, part), y_sem, 3, tm=along(3)),
+    ]
+    for copy in y_copies:
+        copy.start()
+    given = [give(piece(0, 0, share), 0)]
 
     def temporal(block):
         parts = []
@@ -202,6 +247,14 @@
     def _():
         send_back(tm, False)
 
+    def give_out(copies, start, i):
+        for copy in copies:
+            copy.wait_recv()
+        start = pl.multiple_of(start + core * half_width, 16)
+        return give(w_out.at[pl.ds(1, wide - 1), pl.ds(start, half_width)], i)
+
+    given_t = give_out(t_copies, 0, 4)
+
     pltpu.make_async_copy(
         fsend.at[pl.ds(0, 3 * (count - 1))], fsend.at[pl.ds(0, 3 * (count - 1))], f_sem.at[0]
     ).wait()
@@ -216,32 +269,30 @@
         part = fsend.at[pl.ds(0, wide)]
         pltpu.make_async_copy(part, part, f_sem.at[2]).wait()
 
-    loads[2].wait()
-    for copy in gathers[0]:
-        copy.wait()
     most = rrecv.at[:, pl.ds(0, 3 * group)]
     pltpu.make_async_copy(most, most, r_sem.at[1]).wait()
     rest = rrecv.at[:, 3 * group]
     pltpu.make_async_copy(rest, rest, r_sem.at[3]).wait()
+    y_copies[0].wait_recv()
+    y_copies.append(remote(piece(3, 0, part), piece(3, 0, part), y_sem, 4, tm=along(1)))
+    y_copies[4].start()
+    y_copies[1].wait_recv()
+    y_copies.append(remote(piece(1, part, part), piece(1, part, part), y_sem, 5, tm=along(3)))
+    y_copies[5].start()
+    given_s = give_out(s_copies, width, 5)
+    given_t.wait_recv()
     total = own_video
-    for x in range(wide):
-        mixed = dot(order, rrecv[x].reshape(2 * quarter, width)).astype(BF16)
-        total += dot(mixed, w_tout[x])
+    for slot in range(wide):
+        mixed = dot(order, rrecv[peer(slot)].reshape(2 * quarter, width)).astype(BF16)
+        total += dot(mixed, w_out[slot, 0:width])
     x1 = total.astype(BF16).astype(F32)
 
-    def gather(buffer, send, recv):
-        copies = {}
-        for step in (1, 3, 2):
-            copies[step] = pltpu.make_async_remote_copy(
-                buffer.at[hx], buffer.at[hx], send.at[step], recv.at[step],
-                device_id={"heads": peer(step)}, device_id_type=MESH,
-            )
-            copies[step].start()
-        return copies
-
     hbuf[hx] = layer_norm(x1, s_gain[...])
-    copies = gather(hbuf, h_send, h_recv)
-    loads[3].wait()
+    copies = {}
+    for step in (1, 3, 2):
+        copies[step] = remote(hbuf.at[hx], hbuf.at[hx], h_sem, step, heads=peer(step))
+        copies[step].start()
+    loads[6].wait()
     for step in (0, 1, 3, 2):
         if step:
             copies[step].wait_recv()
@@ -249,6 +300,10 @@
         projected = dot_t(hbuf[at], w_sqkv[...].reshape(3 * width, model))
         for f in range(2):
             sqkv[f, at] = projected[f * half : (f + 1) * half]
+    for copy in y_copies[2:4]:
+        copy.wait_recv()
+    given.append(give(piece(3, 0, share), 1))
+    given.append(give(piece(1, 0, share), 2))
     keep = lax.rem(iota((1, wide * half), 1), half) < quarter
     for f in range(2):
         block = sqkv[f].reshape(wide * half, 3 * width).astype(BF16)
@@ -263,49 +318,28 @@
     mix_send[...] = smix[...].reshape(wide, rows, width).astype(BF16)
     mix_copies = []
     for step in (2, 1, 3):
-        copy = pltpu.make_async_remote_copy(
-            mix_send.at[peer(step)], mix_recv.at[hx], x_send.at[step], x_recv.at[step],
-            device_id={"heads": peer(step)}, device_id_type=MESH,
-        )
+        copy = remote(mix_send.at[peer(step)], mix_recv.at[hx], x_sem, step, heads=peer(step))
         copy.start()
         mix_copies.append(copy)
-    loads[4].wait()
-    for copy in gathers[1]:
-        copy.wait()
-    total = x1 + dot(mix_send[hx], w_sout[hx])
+    for copy in y_copies[4:]:
+        copy.wait_recv()
+    given.append(give(piece(2, 0, share), 3))
+    given_s.wait_recv()
+    total = x1 + dot(mix_send[hx], w_out[0, width:])
     for step, copy in zip((2, 1, 3), mix_copies):
         copy.wait_recv()
-        at = peer(wide - step)
-        total += dot(mix_recv[at], w_sout[at])
+        total += dot(mix_recv[peer(wide - step)], w_out[wide - step, width:])
     x2 = total.astype(BF16).astype(F32)
 
-    gbuf[hx] = layer_norm(x2, m_gain[...])
-    g_copies = gather(gbuf, g_send, g_recv)
-    loads[5].wait()
-    loads[6].wait()
-    p_copies = []
-    own_part = None
-    for step in (0, 1, 3, 2):
-        if step:
-            g_copies[step].wait_recv()
-        at = peer(wide - step)
-        up = dot(gbuf[at], w_up[...])
-        hidden = (0.5 * up * (1.0 + lax.erf(up * (0.5 ** 0.5)))).astype(BF16)
-        part = dot(hidden, w_down[...])
-        if step:
-            psend[at] = part.astype(BF16)
-            copy = pltpu.make_async_remote_copy(
-                psend.at[at], precv.at[hx], p_send.at[step], p_recv.at[step],
-                device_id={"heads": at}, device_id_type=MESH,
-            )
-            copy.start()
-            p_copies.append((step, copy))
-        else:
-            own_part = part
-    total = x2 + own_part
-    for step, copy in p_copies:
-        copy.wait_recv()
-        total += precv[peer(step)].astype(F32)
+    normed = layer_norm(x2, m_gain[...])
+    total = x2
+    for slot in range(wide):
+        if slot == 1:
+            for copy in given:
+                copy.wait_recv()
+        up = dot(normed, w_mlp[slot, 0:model])
+        shown = (0.5 * up * (1.0 + lax.erf(up * (0.5 ** 0.5)))).astype(BF16)
+        total += dot(shown, w_mlp[slot, model:])
     for f in range(2):
         block_out[:, f] = total[f * half : f * half + quarter].astype(BF16)
     first = total[:half].astype(BF16)
@@ -358,12 +392,10 @@
         def _():
             pltpu.make_async_copy(rsend_extra, rsend_extra, r_sem.at[2]).wait()
 
-    for step in (1, 2, 3):
-        copies[step].wait_send()
-        g_copies[step].wait_send()
-    for copy in mix_copies:
-        copy.wait_send()
-    for _, copy in p_copies:
+    for copy in (
+        *copies.values(), *mix_copies, *w_copies, *t_copies, *s_copies, *y_copies, *given,
+        given_t, given_s,
+    ):
         copy.wait_send()
 
 
@@ -395,11 +427,9 @@
         scratch_shapes=[
             vmem((positions, frames, model), BF16),
             vmem((3, width, model), BF16),
-            vmem((wide, width, model), BF16),
+            vmem((wide, 2 * width, model), BF16),
             vmem((3, width, model), BF16),
-            vmem((wide, width, model), BF16),
-            vmem((model, hidden), BF16),
-            vmem((hidden, model), BF16),
+            vmem((wide, model + hidden, model), BF16),
             vmem((3, model, model), BF16),
             vmem((positions, 2, 3 * width), BF16),
             vmem((count, 3, 2, 3 * width), BF16),
@@ -412,14 +442,10 @@
             vmem((wide, 2, half, width), F32),
             vmem((wide, rows, width), BF16),
             vmem((wide, rows, width), BF16),
-            vmem((wide, rows, model), BF16),
-            vmem((wide, rows, model), BF16),
-            vmem((wide, rows, model), BF16),
             vmem((edge, model), BF16),
             vmem((edge, model), BF16),
-            dma((8,)), dma((4,)), dma((4,)), dma((4,)), dma((4,)),
-            dma((4,)), dma((4,)), dma((4,)), dma((4,)), dma((4,)), dma((4,)),
-            dma((4,)), dma((4,)), dma((4,)), dma((4,)), dma((2,)),
+            dma((8,)), dma((2, 4)), dma((2, 4)), dma((2, 4)), dma((2, 6)), dma((2, 6)),
+            dma((4,)), dma((4,)), dma((2, 4)), dma((2, 4)), dma((2,)),
         ],
         compiler_params=pltpu.CompilerParams(
             collective_id=0, has_side_effects=True, vmem_limit_bytes=60 * 2**20

time: 88.1 us -> 79.9 us (0.907)
  Pallas kernels: 84.1 us -> 75.9 us
    pallas_call x1, Pallas kernels: 84.1 us -> 75.9 us  [local(): pl.pallas_call(kernel, out_shape=(jax.ShapeDtypeStruct((quarter, frames,...]
where the time goes in v3:
time: 79.9 us; the launch traced here: 79.8 us
  Pallas kernels  75.9 us (95%)
  local copies, waits for them, and re-layouts  3.21 us (4%)
    pallas_call x1, Pallas kernels, local(): pl.pallas_call(kernel, out_shape=(jax.ShapeDtypeStruct((quarter, frames,...  75.9 us
    unnamed x2, local copies, waits for them, and re-layouts  3.21 us

profile of v3, /device:TPU:1, one launch (start us, length us, event | category | flops | bytes accessed | tf_op | source)
XLA Modules:
  0.0 79.8 jit_solution(11436006033168536224)
XLA Ops:
  0.6 75.9 %shard_map.122 = (bf16[49,2,768]{2,1,0:T(2,128)(2,1)}, bf16[1,49,768]{2,1,0:T(8,128)(2,1)}) custom-call(bf16[196,2,768]{2,1,0:T(2,128)(2,1)} %bitcast.2, f32[768]{0:T(1024)} %t_gain.1, bf16[3,192,768]{2,1,0:T(8,128)(2,1)} %t_qkv.1, bf16[192,768]{1,0:T(8,128)(2,1)} %t_out.1, f32[768]{0:T(1024)} %s_gain.1, bf16[3,192,768]{2,1,0:T(8,128)(2,1)} %s_qkv.1, ...), custom_call_target="tpu_custom_call" | custom-call | tf_op jit(solution)/shard_map/pallas_call | solution.py:416
  76.5 1.7 %copy.15 = bf16[2,49,768]{2,0,1:T(2,128)(2,1)} copy(bf16[2,49,768]{2,0,1:T(2,128)(2,1)} %bitcast.3) | data formatting | bytes 301056
  78.2 1.5 %copy.16 = bf16[1,49,768]{2,1,0:T(8,128)(2,1)} copy(bf16[1,49,768]{2,1,0:T(8,128)(2,1)} %get-tuple-element.9) | data formatting | bytes 150528

commit v4 on v3

--- a/solution.py
+++ b/solution.py
@@ -45,7 +45,7 @@
     vid, w_tqkv, w_out, w_sqkv, w_mlp, w_merge,
     fsend, frecv, frecv_extra, rsend, rsend_extra, rrecv,
     hbuf, sqkv, smix, mix_send, mix_recv, edge_send, edge_recv,
-    load_sem, t_sem, s_sem, w_sem, y_sem, c_sem, f_sem, r_sem, h_sem, x_sem, e_sem,
+    load_sem, o_sem, oy_sem, w_sem, y_sem, c_sem, f_sem, r_sem, h_sem, x_sem, e_sem,
 ):
     tm = lax.axis_index("tm")
     hx = lax.axis_index("heads")
@@ -63,7 +63,6 @@
     half = rows // 2
 
     hidden = m_up.shape[1]
-    share = (model + hidden) // 8
     core = lax.rem(tm, 2)
     ring = lax.rem(tm // 2, 4)
 
@@ -139,38 +138,49 @@
     def _():
         pltpu.make_async_copy(fsend.at[own_start + 3], frecv_extra.at[tm], f_sem.at[3]).start()
 
-    def rows_of(step):
-        return (2 * lax.rem(ring + step, 4) + core) * share
-
-    def piece(step, begin, size):
-        start = pl.multiple_of(rows_of(step) + begin, 16)
-        return w_mlp.at[pl.ds(1, wide - 1), pl.ds(start, size)]
-
-    def fetch(buffer, start, size, sems):
-        start = pl.multiple_of(start, 16)
+    others = pl.ds(1, wide - 1)
+
+    def fetch(buffer, rows, sems):
         copies = []
         for step in (2, 1, 3):
             copy = remote(
-                buffer.at[0, pl.ds(start, size)], buffer.at[wide - step, pl.ds(start, size)],
-                sems, step, heads=peer(step),
+                buffer.at[0, rows], buffer.at[wide - step, rows], sems, step, heads=peer(step)
             )
             copy.start()
             copies.append(copy)
         return copies
 
-    def give(block, i):
-        copy = remote(block, block, c_sem, i, tm=tm + 1 - 2 * core)
+    def send(block, sems, i, to):
+        copy = remote(block, block, sems, i, tm=to)
         copy.start()
         return copy
 
-    half_width = width // 2
-    loads[2].wait()
-    loads[3].wait()
-    w_copies = fetch(w_mlp, rows_of(0), share, w_sem)
-    loads[4].wait()
-    t_copies = fetch(w_out, core * half_width, half_width, t_sem)
-    loads[5].wait()
-    s_copies = fetch(w_out, width + core * half_width, half_width, s_sem)
+    out_share = w_out.shape[1] // 8
+    out_cut = out_share // 32 * 16
+
+    def out_rows(step, part):
+        start = (core * 4 + lax.rem(ring + step, 4)) * out_share
+        size = (out_cut, out_share - out_cut, out_share)[part]
+        return pl.ds(pl.multiple_of(start + (out_cut if part == 1 else 0), 16), size)
+
+    def out_block(step, part):
+        return w_out.at[others, out_rows(step, part)]
+
+    mlp_share = w_mlp.shape[1] // 8
+
+    def mlp_rows(step, begin, size):
+        quart = lax.rem(ring + tm // 8 + step, 4)
+        return pl.ds(pl.multiple_of((core * 4 + quart) * mlp_share + begin, 16), size)
+
+    def mlp_block(step, begin, size):
+        return w_mlp.at[others, mlp_rows(step, begin, size)]
+
+    ways = (along(1), along(3), lax.rem(tm + 8, count), lax.rem(tm + count - 8, count))
+    sibling = tm + 1 - 2 * core
+    for i in (2, 3, 4, 5):
+        loads[i].wait()
+    out_x = fetch(w_out, out_rows(0, 2), o_sem)
+    mlp_x = fetch(w_mlp, mlp_rows(0, 0, mlp_share), w_sem)
 
     row = iota((rows, 2 * quarter), 0)
     column = iota((rows, 2 * quarter), 1)
@@ -178,20 +188,20 @@
     order = ((place < quarter) & (column == 2 * place + row // half)).astype(BF16)
     own_video = dot(order, vid[pl.ds(hx * quarter, quarter)].reshape(2 * quarter, model))
 
+    for copy in out_x:
+        copy.wait_recv()
+    out_y = [
+        send(out_block(0, 0), oy_sem, 0, ways[0]),
+        send(out_block(0, 1), oy_sem, 1, ways[1]),
+        send(out_block(0, 1), oy_sem, 2, ways[0]),
+        send(out_block(0, 0), oy_sem, 3, ways[1]),
+    ]
+    out_y[0].wait_recv()
+    out_y.append(send(out_block(3, 0), oy_sem, 4, ways[0]))
+    out_y[1].wait_recv()
+    out_y.append(send(out_block(1, 1), oy_sem, 5, ways[1]))
+
     pltpu.make_async_copy(frecv, frecv, f_sem.at[1]).wait()
-
-    for copy in w_copies:
-        copy.wait_recv()
-    part = share // 2
-    y_copies = [
-        remote(piece(0, 0, part), piece(0, 0, part), y_sem, 0, tm=along(1)),
-        remote(piece(0, part, part), piece(0, part, part), y_sem, 1, tm=along(3)),
-        remote(piece(0, part, part), piece(0, part, part), y_sem, 2, tm=along(1)),
-        remote(piece(0, 0, part), piece(0, 0, part), y_sem, 3, tm=along(3)),
-    ]
-    for copy in y_copies:
-        copy.start()
-    given = [give(piece(0, 0, share), 0)]
 
     def temporal(block):
         parts = []
@@ -247,13 +257,13 @@
     def _():
         send_back(tm, False)
 
-    def give_out(copies, start, i):
-        for copy in copies:
-            copy.wait_recv()
-        start = pl.multiple_of(start + core * half_width, 16)
-        return give(w_out.at[pl.ds(1, wide - 1), pl.ds(start, half_width)], i)
-
-    given_t = give_out(t_copies, 0, 4)
+    for copy in out_y[2:]:
+        copy.wait_recv()
+    half_out = w_out.shape[1] // 2
+    rows_out = pl.ds(pl.multiple_of(core * half_out, 16), half_out)
+    out_given = send(w_out.at[others, rows_out], c_sem, 0, sibling)
+    for copy in mlp_x:
+        copy.wait_recv()
 
     pltpu.make_async_copy(
         fsend.at[pl.ds(0, 3 * (count - 1))], fsend.at[pl.ds(0, 3 * (count - 1))], f_sem.at[0]
@@ -273,14 +283,10 @@
     pltpu.make_async_copy(most, most, r_sem.at[1]).wait()
     rest = rrecv.at[:, 3 * group]
     pltpu.make_async_copy(rest, rest, r_sem.at[3]).wait()
-    y_copies[0].wait_recv()
-    y_copies.append(remote(piece(3, 0, part), piece(3, 0, part), y_sem, 4, tm=along(1)))
-    y_copies[4].start()
-    y_copies[1].wait_recv()
-    y_copies.append(remote(piece(1, part, part), piece(1, part, part), y_sem, 5, tm=along(3)))
-    y_copies[5].start()
-    given_s = give_out(s_copies, width, 5)
-    given_t.wait_recv()
+    part = mlp_share // 2
+    mlp_yz = [send(mlp_block(0, i // 2 * part, part), y_sem, i, ways[i]) for i in range(4)]
+    given = [send(mlp_block(0, 0, mlp_share), c_sem, 1, sibling)]
+    out_given.wait_recv()
     total = own_video
     for slot in range(wide):
         mixed = dot(order, rrecv[peer(slot)].reshape(2 * quarter, width)).astype(BF16)
@@ -294,16 +300,21 @@
         copies[step].start()
     loads[6].wait()
     for step in (0, 1, 3, 2):
+        if step == 2:
+            for copy in mlp_yz:
+                copy.wait_recv()
+            onward = ((3, 1), (1, 0), (3, 3), (1, 2))
+            for i, (whose, place) in enumerate(onward):
+                block = mlp_block(whose, place * (part // 2), part // 2)
+                mlp_yz.append(send(block, y_sem, 4 + i, ways[i]))
         if step:
             copies[step].wait_recv()
         at = peer(wide - step)
         projected = dot_t(hbuf[at], w_sqkv[...].reshape(3 * width, model))
         for f in range(2):
             sqkv[f, at] = projected[f * half : (f + 1) * half]
-    for copy in y_copies[2:4]:
-        copy.wait_recv()
-    given.append(give(piece(3, 0, share), 1))
-    given.append(give(piece(1, 0, share), 2))
+    given.append(send(mlp_block(3, 0, mlp_share), c_sem, 2, sibling))
+    given.append(send(mlp_block(1, 0, mlp_share), c_sem, 3, sibling))
     keep = lax.rem(iota((1, wide * half), 1), half) < quarter
     for f in range(2):
         block = sqkv[f].reshape(wide * half, 3 * width).astype(BF16)
@@ -321,10 +332,9 @@
         copy = remote(mix_send.at[peer(step)], mix_recv.at[hx], x_sem, step, heads=peer(step))
         copy.start()
         mix_copies.append(copy)
-    for copy in y_copies[4:]:
+    for copy in mlp_yz[4:]:
         copy.wait_recv()
-    given.append(give(piece(2, 0, share), 3))
-    given_s.wait_recv()
+    given.append(send(mlp_block(2, 0, mlp_share), c_sem, 4, sibling))
     total = x1 + dot(mix_send[hx], w_out[0, width:])
     for step, copy in zip((2, 1, 3), mix_copies):
         copy.wait_recv()
@@ -393,8 +403,7 @@
             pltpu.make_async_copy(rsend_extra, rsend_extra, r_sem.at[2]).wait()
 
     for copy in (
-        *copies.values(), *mix_copies, *w_copies, *t_copies, *s_copies, *y_copies, *given,
-        given_t, given_s,
+        *copies.values(), *mix_copies, *out_x, *out_y, *mlp_x, *mlp_yz, *given, out_given,
     ):
         copy.wait_send()
 
@@ -444,7 +453,7 @@
             vmem((wide, rows, width), BF16),
             vmem((edge, model), BF16),
             vmem((edge, model), BF16),
-            dma((8,)), dma((2, 4)), dma((2, 4)), dma((2, 4)), dma((2, 6)), dma((2, 6)),
+            dma((8,)), dma((2, 4)), dma((2, 6)), dma((2, 4)), dma((2, 8)), dma((2, 5)),
             dma((4,)), dma((4,)), dma((2, 4)), dma((2, 4)), dma((2,)),
         ],
         compiler_params=pltpu.CompilerParams(

time: 79.9 us -> 70 us (0.88)
  the two profiles are of different devices: /device:TPU:1 before, /device:TPU:32 now
where the time goes in v4:
time: 70 us; the launch traced here: 69.9 us
  Pallas kernels  66 us (94%)
  local copies, waits for them, and re-layouts  3.21 us (5%)
    pallas_call x1, Pallas kernels, local(): pl.pallas_call(kernel, out_shape=(jax.ShapeDtypeStruct((quarter, frames,...  66 us
    unnamed x2, local copies, waits for them, and re-layouts  3.21 us

profile of v4, /device:TPU:32, one launch (start us, length us, event | category | flops | bytes accessed | tf_op | source)
XLA Modules:
  0.0 69.9 jit_solution(4999210444936503424)
XLA Ops:
  0.6 66.0 %shard_map.122 = (bf16[49,2,768]{2,1,0:T(2,128)(2,1)}, bf16[1,49,768]{2,1,0:T(8,128)(2,1)}) custom-call(bf16[196,2,768]{2,1,0:T(2,128)(2,1)} %bitcast.2, f32[768]{0:T(1024)} %t_gain.1, bf16[3,192,768]{2,1,0:T(8,128)(2,1)} %t_qkv.1, bf16[192,768]{1,0:T(8,128)(2,1)} %t_out.1, f32[768]{0:T(1024)} %s_gain.1, bf16[3,192,768]{2,1,0:T(8,128)(2,1)} %s_qkv.1, ...), custom_call_target="tpu_custom_call" | custom-call | tf_op jit(solution)/shard_map/pallas_call | solution.py:425
  66.7 1.7 %copy.15 = bf16[2,49,768]{2,0,1:T(2,128)(2,1)} copy(bf16[2,49,768]{2,0,1:T(2,128)(2,1)} %bitcast.3) | data formatting | bytes 301056
  68.3 1.5 %copy.16 = bf16[1,49,768]{2,1,0:T(8,128)(2,1)} copy(bf16[1,49,768]{2,1,0:T(8,128)(2,1)} %get-tuple-element.9) | data formatting | bytes 150528

commit v5 on v4

--- a/solution.py
+++ b/solution.py
@@ -140,11 +140,12 @@
 
     others = pl.ds(1, wide - 1)
 
-    def fetch(buffer, rows, sems):
+    def fetch(buffer, rows, sems, base=0):
         copies = []
         for step in (2, 1, 3):
             copy = remote(
-                buffer.at[0, rows], buffer.at[wide - step, rows], sems, step, heads=peer(step)
+                buffer.at[0, rows], buffer.at[wide - step, rows], sems, base + step,
+                heads=peer(step),
             )
             copy.start()
             copies.append(copy)
@@ -180,7 +181,9 @@
     for i in (2, 3, 4, 5):
         loads[i].wait()
     out_x = fetch(w_out, out_rows(0, 2), o_sem)
-    mlp_x = fetch(w_mlp, mlp_rows(0, 0, mlp_share), w_sem)
+    third = mlp_share // 3
+    mlp_x = fetch(w_mlp, mlp_rows(0, 0, third), w_sem)
+    mlp_x += fetch(w_mlp, mlp_rows(0, third, 2 * third), w_sem, 4)
 
     row = iota((rows, 2 * quarter), 0)
     column = iota((rows, 2 * quarter), 1)
@@ -200,6 +203,9 @@
     out_y.append(send(out_block(3, 0), oy_sem, 4, ways[0]))
     out_y[1].wait_recv()
     out_y.append(send(out_block(1, 1), oy_sem, 5, ways[1]))
+    for copy in mlp_x[:3]:
+        copy.wait_recv()
+    mlp_yz = [send(mlp_block(0, 0, third), y_sem, 8 + i, ways[i]) for i in range(2)]
 
     pltpu.make_async_copy(frecv, frecv, f_sem.at[1]).wait()
 
@@ -262,7 +268,7 @@
     half_out = w_out.shape[1] // 2
     rows_out = pl.ds(pl.multiple_of(core * half_out, 16), half_out)
     out_given = send(w_out.at[others, rows_out], c_sem, 0, sibling)
-    for copy in mlp_x:
+    for copy in mlp_x[3:]:
         copy.wait_recv()
 
     pltpu.make_async_copy(
@@ -283,8 +289,10 @@
     pltpu.make_async_copy(most, most, r_sem.at[1]).wait()
     rest = rrecv.at[:, 3 * group]
     pltpu.make_async_copy(rest, rest, r_sem.at[3]).wait()
-    part = mlp_share // 2
-    mlp_yz = [send(mlp_block(0, i // 2 * part, part), y_sem, i, ways[i]) for i in range(4)]
+    mlp_yz += [
+        send(mlp_block(0, (1 + i // 2) * third, third), y_sem, i, ways[i]) for i in range(4)
+    ]
+    part = mlp_share // 4
     given = [send(mlp_block(0, 0, mlp_share), c_sem, 1, sibling)]
     out_given.wait_recv()
     total = own_video
@@ -294,10 +302,20 @@
     x1 = total.astype(BF16).astype(F32)
 
     hbuf[hx] = layer_norm(x1, s_gain[...])
-    copies = {}
-    for step in (1, 3, 2):
-        copies[step] = remote(hbuf.at[hx], hbuf.at[hx], h_sem, step, heads=peer(step))
-        copies[step].start()
+    upper, lower = pl.ds(0, rows // 32 * 16), pl.ds(rows // 32 * 16, rows - rows // 32 * 16)
+
+    def pass_on(whose, part, i, step):
+        block = hbuf.at[whose, part]
+        copy = remote(block, block, h_sem, i, heads=peer(step))
+        copy.start()
+        return copy
+
+    copies = [
+        pass_on(hx, upper, 0, 1),
+        pass_on(hx, lower, 1, 3),
+        pass_on(hx, lower, 2, 1),
+        pass_on(hx, upper, 3, 3),
+    ]
     loads[6].wait()
     for step in (0, 1, 3, 2):
         if step == 2:
@@ -305,16 +323,21 @@
                 copy.wait_recv()
             onward = ((3, 1), (1, 0), (3, 3), (1, 2))
             for i, (whose, place) in enumerate(onward):
-                block = mlp_block(whose, place * (part // 2), part // 2)
+                block = mlp_block(whose, place * part, part)
                 mlp_yz.append(send(block, y_sem, 4 + i, ways[i]))
-        if step:
-            copies[step].wait_recv()
+            given.append(send(mlp_block(3, 0, mlp_share), c_sem, 2, sibling))
+            given.append(send(mlp_block(1, 0, mlp_share), c_sem, 3, sibling))
+        if step == 1:
+            copies[0].wait_recv()
+            copies.append(pass_on(peer(3), upper, 4, 1))
+            copies[1].wait_recv()
+            copies.append(pass_on(peer(1), lower, 5, 3))
+        for i in ((), (2,), (4, 5), (3,))[step]:
+            copies[i].wait_recv()
         at = peer(wide - step)
         projected = dot_t(hbuf[at], w_sqkv[...].reshape(3 * width, model))
         for f in range(2):
             sqkv[f, at] = projected[f * half : (f + 1) * half]
-    given.append(send(mlp_block(3, 0, mlp_share), c_sem, 2, sibling))
-    given.append(send(mlp_block(1, 0, mlp_share), c_sem, 3, sibling))
     keep = lax.rem(iota((1, wide * half), 1), half) < quarter
     for f in range(2):
         block = sqkv[f].reshape(wide * half, 3 * width).astype(BF16)
@@ -332,7 +355,7 @@
         copy = remote(mix_send.at[peer(step)], mix_recv.at[hx], x_sem, step, heads=peer(step))
         copy.start()
         mix_copies.append(copy)
-    for copy in mlp_yz[4:]:
+    for copy in mlp_yz[6:]:
         copy.wait_recv()
     given.append(send(mlp_block(2, 0, mlp_share), c_sem, 4, sibling))
     total = x1 + dot(mix_send[hx], w_out[0, width:])
@@ -403,7 +426,7 @@
             pltpu.make_async_copy(rsend_extra, rsend_extra, r_sem.at[2]).wait()
 
     for copy in (
-        *copies.values(), *mix_copies, *out_x, *out_y, *mlp_x, *mlp_yz, *given, out_given,
+        *copies, *mix_copies, *out_x, *out_y, *mlp_x, *mlp_yz, *given, out_given,
     ):
         copy.wait_send()
 
@@ -453,11 +476,11 @@
             vmem((wide, rows, width), BF16),
             vmem((edge, model), BF16),
             vmem((edge, model), BF16),
-            dma((8,)), dma((2, 4)), dma((2, 6)), dma((2, 4)), dma((2, 8)), dma((2, 5)),
-            dma((4,)), dma((4,)), dma((2, 4)), dma((2, 4)), dma((2,)),
+            dma((8,)), dma((2, 4)), dma((2, 6)), dma((2, 8)), dma((2, 10)), dma((2, 5)),
+            dma((4,)), dma((4,)), dma((2, 6)), dma((2, 4)), dma((2,)),
         ],
         compiler_params=pltpu.CompilerParams(
-            collective_id=0, has_side_effects=True, vmem_limit_bytes=60 * 2**20
+            collective_id=0, has_side_effects=True, vmem_limit_bytes=107 * 2**19
         ),
     )(
         jnp.swapaxes(video, 0, 1), t_gain, t_qkv, t_out, s_gain, s_qkv, s_out, m_gain,

time: 70 us -> 67.2 us (0.960)
  the two profiles are of different devices: /device:TPU:32 before, /device:TPU:1 now
where the time goes in v5:
time: 67.2 us; the launch traced here: 66.3 us
  Pallas kernels  62.3 us (93%)
  local copies, waits for them, and re-layouts  3.35 us (5%)
    pallas_call x1, Pallas kernels, local(): pl.pallas_call(kernel, out_shape=(jax.ShapeDtypeStruct((quarter, frames,...  62.3 us
    unnamed x8, local copies, waits for them, and re-layouts  3.35 us

profile of v5, /device:TPU:1, one launch (start us, length us, event | category | flops | bytes accessed | tf_op | source)
XLA Modules:
  0.0 66.3 jit_solution(3768164825527386630)
XLA Ops:
  0.6 0.0 copy-start
  0.6 0.7 %copy-done = f32[768]{0:T(1024)S(1)} copy-done((f32[768]{0:T(1024)S(1)}, f32[768]{0:T(1024)}, u32[]{:S(2)}) %copy-start) | copy-done | bytes 3096
  1.3 0.0 copy-start.1
  1.3 0.7 %copy-done.1 = f32[768]{0:T(1024)S(1)} copy-done((f32[768]{0:T(1024)S(1)}, f32[768]{0:T(1024)}, u32[]{:S(2)}) %copy-start.1) | copy-done | bytes 3096
  2.0 0.0 copy-start.2
  2.0 0.7 %copy-done.2 = f32[768]{0:T(1024)S(1)} copy-done((f32[768]{0:T(1024)S(1)}, f32[768]{0:T(1024)}, u32[]{:S(2)}) %copy-start.2) | copy-done | bytes 3096
  2.7 62.3 %shard_map.122 = (bf16[49,2,768]{2,1,0:T(2,128)(2,1)S(1)}, bf16[1,49,768]{2,1,0:T(8,128)(2,1)S(1)}) custom-call(bf16[196,2,768]{2,1,0:T(2,128)(2,1)} %bitcast.3, f32[768]{0:T(1024)S(1)} %copy-done, bf16[3,192,768]{2,1,0:T(8,128)(2,1)} %t_qkv.1, bf16[192,768]{1,0:T(8,128)(2,1)} %t_out.1, f32[768]{0:T(1024)S(1)} %copy-done.1, bf16[3,192,768]{2,1,0:T(8,128)(2,1)} %s_qkv.1, ...), custom_call_target="tpu_custom_call" | custom-call | tf_op jit(solution)/shard_map/pallas_call | solution.py:448
  65.0 0.7 %copy.15 = bf16[2,49,768]{2,0,1:T(2,128)(2,1)} copy(bf16[2,49,768]{2,0,1:T(2,128)(2,1)S(1)} %bitcast.2) | data formatting | bytes 301056
  65.7 0.6 copy.16
Async XLA Ops:
  0.6 0.7 %copy-start = (f32[768]{0:T(1024)S(1)}, f32[768]{0:T(1024)}, u32[]{:S(2)}) copy-start(f32[768]{0:T(1024)} %t_gain.1) | copy-start | bytes 9220
  1.3 0.7 %copy-start.1 = (f32[768]{0:T(1024)S(1)}, f32[768]{0:T(1024)}, u32[]{:S(2)}) copy-start(f32[768]{0:T(1024)} %s_gain.1) | copy-start | bytes 9220
  2.0 0.7 %copy-start.2 = (f32[768]{0:T(1024)S(1)}, f32[768]{0:T(1024)}, u32[]{:S(2)}) copy-start(f32[768]{0:T(1024)} %m_gain.1) | copy-start | bytes 9220

commit v6 on v5

--- a/solution.py
+++ b/solution.py
@@ -115,29 +115,6 @@
     def first_position(device):
         return (device // group) * quarter + lax.rem(device, group) * 3
 
-    @pl.loop(0, count - 1)
-    def _(k):
-        to = other(k)
-        start = first_position(to)
-        pltpu.make_async_remote_copy(
-            fsend.at[pl.ds(start, 3)], frecv.at[tm], f_sem.at[0], f_sem.at[1],
-            device_id={"tm": to}, device_id_type=MESH,
-        ).start()
-
-        @pl.when(lax.rem(to, group) == group - 1)
-        def _():
-            pltpu.make_async_remote_copy(
-                fsend.at[start + 3], frecv_extra.at[tm], f_sem.at[2], f_sem.at[3],
-                device_id={"tm": to}, device_id_type=MESH,
-            ).start()
-
-    own_start = first_position(tm)
-    pltpu.make_async_copy(fsend.at[pl.ds(own_start, 3)], frecv.at[tm], f_sem.at[1]).start()
-
-    @pl.when(last)
-    def _():
-        pltpu.make_async_copy(fsend.at[own_start + 3], frecv_extra.at[tm], f_sem.at[3]).start()
-
     others = pl.ds(1, wide - 1)
 
     def fetch(buffer, rows, sems, base=0):
@@ -184,6 +161,29 @@
     third = mlp_share // 3
     mlp_x = fetch(w_mlp, mlp_rows(0, 0, third), w_sem)
     mlp_x += fetch(w_mlp, mlp_rows(0, third, 2 * third), w_sem, 4)
+
+    @pl.loop(0, count - 1)
+    def _(k):
+        to = other(k)
+        start = first_position(to)
+        pltpu.make_async_remote_copy(
+            fsend.at[pl.ds(start, 3)], frecv.at[tm], f_sem.at[0], f_sem.at[1],
+            device_id={"tm": to}, device_id_type=MESH,
+        ).start()
+
+        @pl.when(lax.rem(to, group) == group - 1)
+        def _():
+            pltpu.make_async_remote_copy(
+                fsend.at[start + 3], frecv_extra.at[tm], f_sem.at[2], f_sem.at[3],
+                device_id={"tm": to}, device_id_type=MESH,
+            ).start()
+
+    own_start = first_position(tm)
+    pltpu.make_async_copy(fsend.at[pl.ds(own_start, 3)], frecv.at[tm], f_sem.at[1]).start()
+
+    @pl.when(last)
+    def _():
+        pltpu.make_async_copy(fsend.at[own_start + 3], frecv_extra.at[tm], f_sem.at[3]).start()
 
     row = iota((rows, 2 * quarter), 0)
     column = iota((rows, 2 * quarter), 1)

time: 67.2 us -> 65.8 us (0.979)
  Pallas kernels: 62.3 us -> 61.1 us
    pallas_call x1, Pallas kernels: 62.3 us -> 61.1 us  [local(): pl.pallas_call(kernel, out_shape=(jax.ShapeDtypeStruct((quarter, frames,...]
where the time goes in v6:
time: 65.8 us; the launch traced here: 65.1 us
  Pallas kernels  61.1 us (93%)
  local copies, waits for them, and re-layouts  3.35 us (5%)
    pallas_call x1, Pallas kernels, local(): pl.pallas_call(kernel, out_shape=(jax.ShapeDtypeStruct((quarter, frames,...  61.1 us
    unnamed x8, local copies, waits for them, and re-layouts  3.35 us

profile of v6, /device:TPU:1, one launch (start us, length us, event | category | flops | bytes accessed | tf_op | source)
XLA Modules:
  0.0 65.1 jit_solution(17831276967532031691)
XLA Ops:
  0.6 0.0 copy-start
  0.6 0.7 %copy-done = f32[768]{0:T(1024)S(1)} copy-done((f32[768]{0:T(1024)S(1)}, f32[768]{0:T(1024)}, u32[]{:S(2)}) %copy-start) | copy-done | bytes 3096
  1.3 0.0 copy-start.1
  1.3 0.7 %copy-done.1 = f32[768]{0:T(1024)S(1)} copy-done((f32[768]{0:T(1024)S(1)}, f32[768]{0:T(1024)}, u32[]{:S(2)}) %copy-start.1) | copy-done | bytes 3096
  2.0 0.0 copy-start.2
  2.0 0.7 %copy-done.2 = f32[768]{0:T(1024)S(1)} copy-done((f32[768]{0:T(1024)S(1)}, f32[768]{0:T(1024)}, u32[]{:S(2)}) %copy-start.2) | copy-done | bytes 3096
  2.7 61.1 %shard_map.122 = (bf16[49,2,768]{2,1,0:T(2,128)(2,1)S(1)}, bf16[1,49,768]{2,1,0:T(8,128)(2,1)S(1)}) custom-call(bf16[196,2,768]{2,1,0:T(2,128)(2,1)} %bitcast.3, f32[768]{0:T(1024)S(1)} %copy-done, bf16[3,192,768]{2,1,0:T(8,128)(2,1)} %t_qkv.1, bf16[192,768]{1,0:T(8,128)(2,1)} %t_out.1, f32[768]{0:T(1024)S(1)} %copy-done.1, bf16[3,192,768]{2,1,0:T(8,128)(2,1)} %s_qkv.1, ...), custom_call_target="tpu_custom_call" | custom-call | tf_op jit(solution)/shard_map/pallas_call | solution.py:448
  63.8 0.7 %copy.15 = bf16[2,49,768]{2,0,1:T(2,128)(2,1)} copy(bf16[2,49,768]{2,0,1:T(2,128)(2,1)S(1)} %bitcast.2) | data formatting | bytes 301056
  64.4 0.6 copy.16
Async XLA Ops:
  0.6 0.7 %copy-start = (f32[768]{0:T(1024)S(1)}, f32[768]{0:T(1024)}, u32[]{:S(2)}) copy-start(f32[768]{0:T(1024)} %t_gain.1) | copy-start | bytes 9220
  1.3 0.7 %copy-start.1 = (f32[768]{0:T(1024)S(1)}, f32[768]{0:T(1024)}, u32[]{:S(2)}) copy-start(f32[768]{0:T(1024)} %s_gain.1) | copy-start | bytes 9220
  2.0 0.7 %copy-start.2 = (f32[768]{0:T(1024)S(1)}, f32[768]{0:T(1024)}, u32[]{:S(2)}) copy-start(f32[768]{0:T(1024)} %m_gain.1) | copy-start | bytes 9220

commit v7 on v6

--- a/solution.py
+++ b/solution.py
@@ -31,7 +31,7 @@
 
 
 def attend(queries, keys, values, valid):
-    scores = dot_t(queries, keys) * (HD ** -0.5)
+    scores = dot_t(queries * BF16(HD ** -0.5), keys)
     if valid is not None:
         scores = jnp.where(valid, scores, -jnp.inf)
     raised = jnp.exp(scores - jnp.max(scores, axis=-1, keepdims=True))

time: 65.8 us -> 65.8 us (level)
  no operation moved by 1% of the time
where the time goes in v7:
time: 65.8 us; the launch traced here: 65.1 us
  Pallas kernels  61.1 us (93%)
  local copies, waits for them, and re-layouts  3.35 us (5%)
    pallas_call x1, Pallas kernels, local(): pl.pallas_call(kernel, out_shape=(jax.ShapeDtypeStruct((quarter, frames,...  61.1 us
    unnamed x8, local copies, waits for them, and re-layouts  3.35 us

profile of v7, /device:TPU:1, one launch (start us, length us, event | category | flops | bytes accessed | tf_op | source)
XLA Modules:
  0.0 65.1 jit_solution(3078082035214928632)
XLA Ops:
  0.6 0.0 copy-start
  0.6 0.7 %copy-done = f32[768]{0:T(1024)S(1)} copy-done((f32[768]{0:T(1024)S(1)}, f32[768]{0:T(1024)}, u32[]{:S(2)}) %copy-start) | copy-done | bytes 3096
  1.3 0.0 copy-start.1
  1.3 0.7 %copy-done.1 = f32[768]{0:T(1024)S(1)} copy-done((f32[768]{0:T(1024)S(1)}, f32[768]{0:T(1024)}, u32[]{:S(2)}) %copy-start.1) | copy-done | bytes 3096
  2.0 0.0 copy-start.2
  2.0 0.7 %copy-done.2 = f32[768]{0:T(1024)S(1)} copy-done((f32[768]{0:T(1024)S(1)}, f32[768]{0:T(1024)}, u32[]{:S(2)}) %copy-start.2) | copy-done | bytes 3096
  2.7 61.1 %shard_map.122 = (bf16[49,2,768]{2,1,0:T(2,128)(2,1)S(1)}, bf16[1,49,768]{2,1,0:T(8,128)(2,1)S(1)}) custom-call(bf16[196,2,768]{2,1,0:T(2,128)(2,1)} %bitcast.3, f32[768]{0:T(1024)S(1)} %copy-done, bf16[3,192,768]{2,1,0:T(8,128)(2,1)} %t_qkv.1, bf16[192,768]{1,0:T(8,128)(2,1)} %t_out.1, f32[768]{0:T(1024)S(1)} %copy-done.1, bf16[3,192,768]{2,1,0:T(8,128)(2,1)} %s_qkv.1, ...), custom_call_target="tpu_custom_call" | custom-call | tf_op jit(solution)/shard_map/pallas_call | solution.py:448
  63.8 0.7 %copy.15 = bf16[2,49,768]{2,0,1:T(2,128)(2,1)} copy(bf16[2,49,768]{2,0,1:T(2,128)(2,1)S(1)} %bitcast.2) | data formatting | bytes 301056
  64.5 0.6 copy.16
Async XLA Ops:
  0.6 0.7 %copy-start = (f32[768]{0:T(1024)S(1)}, f32[768]{0:T(1024)}, u32[]{:S(2)}) copy-start(f32[768]{0:T(1024)} %t_gain.1) | copy-start | bytes 9220
  1.3 0.7 %copy-start.1 = (f32[768]{0:T(1024)S(1)}, f32[768]{0:T(1024)}, u32[]{:S(2)}) copy-start(f32[768]{0:T(1024)} %s_gain.1) | copy-start | bytes 9220
  2.0 0.7 %copy-start.2 = (f32[768]{0:T(1024)S(1)}, f32[768]{0:T(1024)}, u32[]{:S(2)}) copy-start(f32[768]{0:T(1024)} %m_gain.1) | copy-start | bytes 9220
